TPU v7x, 1024 devices: a whole 4x8x16 slice. The times are simulated.
1024 devices in a mesh: dp: 32 (over z, core), owner: 32 (over y, x).
Axes of the slice: x: 4, y: 8, z: 16, core: 2. Of those that a mesh axis runs over, the one named last changes fastest.
Arguments:
- acts: bfloat16 [32768, 4096], P('dp'), may hold values from -33 to 33
- dout: bfloat16 [32768, 8, 512], P('dp', None, 'owner'), may hold values from -2 to 2
- left_stats: float32 [128, 512, 512], P('owner', 'dp'), may hold values from -3 to 3
- right_stats: float32 [128, 512, 512], P('owner', 'dp'), may hold values from -3 to 3
- left_root: bfloat16 [128, 512, 512], P('owner', 'dp'), may hold values from -10 to 10
- right_root: bfloat16 [128, 512, 512], P('owner'), may hold values from -10 to 10
- owner_of: int32 [64, 1], replicated, may hold values from 0 to 31; in each aligned block of 64 rows (0 to 63, 64 to 127, ...) at most 4 rows name the same one
- counters: int32 [64], replicated, may hold values from 0 to 49
Outputs:
- left_out: float32 [128, 512, 512], P('owner', 'dp')
- right_out: float32 [128, 512, 512], P('owner', 'dp')
- update: bfloat16 [8, 512, 8, 512], P(None, 'dp', None, 'owner')
Inputs may be any that keep to these rules, and one draw needn't show every extreme that they name: `owner_of`: every owner owns at least one block and at most 4; some owner owns exactly 4.
All inputs are finite; a program needn't handle non-finite values.
Results may differ from a plain program's by a relative error of at most 0.009.
Values may be sent and summed in bfloat16 or wider, within the bound.
A program may use at most 64 MiB of HBM per device.

v0:
```python
import jax
import jax.numpy as jnp
from jax import lax
from jax.sharding import PartitionSpec as P

WARMUP = 25


decay_rate = 0.95
epsilon = 1e-06


def slot_table(owner_of):
    owners = owner_of[:, 0]
    total = owners.shape[0]
    same_owner = owners[None, :] == owners[:, None]
    ordinal = jnp.arange(total, dtype=jnp.int32)
    earlier = ordinal[None, :] < ordinal[:, None]
    return (owners, jnp.sum((same_owner & earlier).astype(jnp.int32), axis=1))


def on_device(acts, dout, left_stats, right_stats, left_root, right_root, owner_of, counters):
    owner_size = lax.axis_size("owner")
    dp_index = lax.axis_index("dp")
    owner_index = lax.axis_index("owner")
    tokens, features = acts.shape
    col_blocks, col_share = (dout.shape[1], dout.shape[2])
    slot_count, row_share, block_order = left_stats.shape
    row_blocks = features // block_order
    block_total = row_blocks * col_blocks
    piece_rows = row_blocks * row_share
    tile_size = row_share * col_share
    col_total = col_blocks * col_share
    my_dout = dout.reshape(tokens, col_total)
    acts_grid = acts.reshape(tokens, row_blocks, block_order)
    spread = lax.axis_size("dp") * piece_rows // piece_rows
    columns = acts_grid
    columns = (
        columns.reshape(tokens, row_blocks, spread, row_share)
        .transpose(0, 2, 1, 3)
        .reshape(tokens, lax.axis_size("dp") * piece_rows)
    )
    summed = lax.psum_scatter(
        lax.dot_general(
            columns, my_dout, (((0,), (0,)), ((), ())), preferred_element_type=jnp.float32
        ),
        "dp",
        scatter_dimension=0,
        tiled=True,
    )
    gradient = summed.astype(jnp.bfloat16)
    grad_tiles = (
        gradient.reshape(row_blocks, row_share, col_blocks, col_share)
        .transpose(0, 2, 1, 3)
        .reshape(block_total, tile_size)
    )
    owners, slot_of = slot_table(owner_of)
    destination = owners * slot_count + slot_of
    outgoing = (
        jnp.zeros((owner_size * slot_count, tile_size), jnp.bfloat16)
        .at[destination]
        .set(grad_tiles)
    )
    incoming = lax.all_to_all(
        outgoing.reshape(owner_size, slot_count, tile_size),
        "owner",
        split_axis=0,
        concat_axis=0,
        tiled=True,
    )
    own_grad = (
        incoming.reshape(owner_size, slot_count, row_share, col_share)
        .transpose(1, 2, 0, 3)
        .reshape(slot_count, row_share, block_order)
    )
    row_start = dp_index * row_share
    shard_rows = lax.all_gather(own_grad, "dp", axis=1, tiled=True)
    left_cols = jnp.einsum("srk,sck->src", own_grad, shard_rows, preferred_element_type=jnp.float32)
    own_cols = lax.dynamic_slice_in_dim(shard_rows, row_start, row_share, 2)
    right_acc = jnp.einsum("skr,skc->src", own_cols, shard_rows, preferred_element_type=jnp.float32)
    inner_acc = jnp.einsum(
        "srk,skc->src", left_root, shard_rows, preferred_element_type=jnp.float32
    )
    precise = shard_rows.astype(jnp.float32)
    result_totals = (left_cols, right_acc, inner_acc, jnp.sum(precise * precise, axis=(1, 2)))
    left_out = decay_rate * left_stats + (1.0 - decay_rate) * result_totals[0]
    right_out = decay_rate * right_stats + (1.0 - decay_rate) * result_totals[1]
    precond = jnp.einsum(
        "src,sce->sre",
        result_totals[2].astype(jnp.bfloat16),
        right_root,
        preferred_element_type=jnp.float32,
    ).astype(jnp.bfloat16)
    owned_here = owners == owner_index
    slot_ids = jnp.arange(slot_count, dtype=jnp.int32)
    slot_hit = (slot_of[None, :] == slot_ids[:, None]) & owned_here[None, :]
    started = jnp.any(slot_hit & (counters[None, :] >= WARMUP), axis=1)
    precise = precond.astype(jnp.float32)
    pre_sq = lax.psum(jnp.sum(precise * precise, axis=(1, 2)), "dp")
    graft_scale = jnp.sqrt(result_totals[3] / (pre_sq + epsilon))
    result = jnp.where(
        started[:, None, None],
        (precise * graft_scale[:, None, None]).astype(jnp.bfloat16),
        own_grad,
    )
    gathered = lax.all_gather(result, "owner", axis=0, tiled=True)
    column_part = lax.dynamic_slice_in_dim(gathered, owner_index * col_share, col_share, 2)
    returned = column_part.reshape(owner_size * slot_count, tile_size)[destination]
    update = returned.reshape(row_blocks, col_blocks, row_share, col_share).transpose(0, 2, 1, 3)
    return (left_out, right_out, update)


def solution(mesh):
    in_specs = (
        P("dp", None),
        P("dp", None, "owner"),
        P("owner", "dp", None),
        P("owner", "dp", None),
        P("owner", "dp", None),
        P("owner", None, None),
        P(),
        P(),
    )
    out_specs = (P("owner", "dp", None), P("owner", "dp", None), P(None, "dp", None, "owner"))
    return jax.shard_map(
        on_device, mesh=mesh, in_specs=in_specs, out_specs=out_specs, check_vma=False
    )
```

profile of v0, /device:TPU:1, one launch (start us, length us, event | category | flops | bytes accessed | tf_op | source)
XLA Modules:
  0.0 396.6 jit_solution(18075005813851066198)
XLA Ops:
  7.2 12.1 %copy.39 = bf16[1024,4096]{0,1:T(8,128)(2,1)} copy(bf16[1024,4096]{1,0:T(8,128)(2,1)} %param.8) | data formatting | bytes 16777216 | tf_op args[0]
  19.3 8.6 %copy.40 = bf16[1024,32,8,16]{0,3,2,1:T(8,128)(2,1)} copy(bf16[1024,32,8,16]{0,3,1,2:T(8,128)(2,1)} %bitcast.36) | data formatting | bytes 16777216 | tf_op jit(solution)/shard_map/transpose | solution.py:40
  27.9 7.1 %fusion.14 = f32[4096,128]{1,0:T(8,128)} fusion(bf16[1024,4096]{0,1:T(8,128)(2,1)} %bitcast.35, bf16[1024,128]{0,1:T(8,128)(2,1)S(1)} %bitcast.39), kind=kOutput, calls=%fused_computation.35 | convolution fusion | flops 1073741824 | bytes 10747904 | tf_op jit(solution)/shard_map/dot_general | solution.py:44
  35.1 0.6 copy-done.7
  35.8 119.5 %reduce-scatter.2.cloned.1.call-done = f32[128,128]{1,0:T(8,128)} async-done(((f32[4096,128]{1,0:T(8,128)}), f32[128,128]{1,0:T(8,128)}) %reduce-scatter.2.cloned.1.call-update) | async-done | bytes 65552 | tf_op jit(solution)/shard_map/reduce_scatter | solution.py:43
  155.3 0.8 convert_element_type.23
  156.4 0.2 reshape.66
  156.6 0.8 scatter_custom_fusion
  157.5 17.8 %all_to_all.5 = bf16[32,4,256]{2,1,0:T(4,128)(2,1)S(1)} all-to-all(bf16[32,4,256]{2,1,0:T(4,128)(2,1)S(1)} %reshape.49), channel_id=1, replica_groups=mesh['dp'=32,'owner'=32] {'owner'}, dimensions={0} | all-to-all | bytes 131072 | tf_op jit(solution)/shard_map/all_to_all | solution.py:64
  175.5 0.3 copy.43
  175.8 1.4 reshape.51
  177.4 70.2 %all-gather.3.cloned.1.call-done = bf16[4,512,512]{2,1,0:T(8,128)(2,1)} async-done(((bf16[4,16,512]{2,1,0:T(8,128)(2,1)}), bf16[4,512,512]{2,1,0:T(8,128)(2,1)}) %all-gather.3.cloned.1.call-update) | async-done | bytes 2097168 | tf_op jit(solution)/shard_map/all_gather | solution.py:77
  247.7 2.3 multiply_reduce_fusion.1
  250.0 45.5 %psum.7 = f32[4]{0:T(128)S(1)} all-reduce(f32[4]{0:T(128)S(1)} %get-tuple-element.3), channel_id=1, replica_groups=mesh['dp'=32,'owner'=32] {'dp'}, use_global_device_ids=true, to_apply=%region_6.0 | all-reduce | flops 4 | bytes 32 | tf_op jit(solution)/shard_map/psum | solution.py:99
  295.5 2.3 multiply_reduce_fusion
  297.8 0.7 fusion.4
  298.6 3.2 fusion
  301.8 1.3 fusion.1
  303.1 83.5 %all-gather.5.cloned.1.call-done = bf16[128,16,512]{2,1,0:T(8,128)(2,1)} async-done(((bf16[4,16,512]{2,1,0:T(8,128)(2,1)}), bf16[128,16,512]{2,1,0:T(8,128)(2,1)}) %all-gather.5.cloned.1.call-update) | async-done | bytes 2097168 | tf_op jit(solution)/shard_map/all_gather | solution.py:106
  386.6 1.2 constant_dynamic-slice_fusion
  387.8 0.4 copy.49
  388.4 0.7 gather_fusion
  389.1 0.2 reshape.53
  389.3 0.8 copy.52
  (35 shorter events, 1.1 us)
Async XLA Ops:
  7.2 240.5 %copy-start = (bf16[4,512,512]{2,1,0:T(8,128)(2,1)S(1)}, bf16[4,512,512]{2,1,0:T(8,128)(2,1)}, u32[]{:S(2)}) copy-start(bf16[4,512,512]{2,1,0:T(8,128)(2,1)} %param.13) | copy-start | bytes 6291460
  7.2 148.1 %reduce-scatter.2.cloned.1.call-start = ((), (), s32[]{:S(2)}) async-start(), calls=%async_computation.2 | async-start | bytes 2162688 | tf_op jit(solution)/shard_map/reduce_scatter | solution.py:43
  19.3 8.6 %copy-start.3 = (bf16[1024,8,16]{0,2,1:T(8,128)(2,1)S(1)}, bf16[1024,8,16]{0,2,1:T(8,128)(2,1)}, u32[]{:S(2)}) copy-start(bf16[1024,8,16]{0,2,1:T(8,128)(2,1)} %param.9) | copy-start | bytes 786436
  35.0 0.7 copy-start.7
  35.0 142.3 %copy-start.8 = (s32[64]{0:T(128)S(1)}, s32[64]{0:T(128)}, u32[]{:S(2)}) copy-start(s32[64]{0:T(128)} %param.15) | copy-start | bytes 772
  35.0 212.6 %copy-start.6 = (bf16[4,16,512]{2,1,0:T(8,128)(2,1)S(1)}, bf16[4,16,512]{2,1,0:T(8,128)(2,1)}, u32[]{:S(2)}) copy-start(bf16[4,16,512]{2,1,0:T(8,128)(2,1)} %param.12) | copy-start | bytes 196612
  35.0 212.6 %all-gather.3.cloned.1.call-start = ((), (), s32[]{:S(2)}) async-start(), calls=%async_computation.3 | async-start | bytes 2162688 | tf_op jit(solution)/shard_map/all_gather | solution.py:77
  177.2 209.4 %all-gather.5.cloned.1.call-start = ((), (), s32[]{:S(2)}) async-start(), calls=%async_computation.4 | async-start | bytes 2162688 | tf_op jit(solution)/shard_map/all_gather | solution.py:106
  250.0 47.8 %copy-start.2 = (bf16[4,16,512]{2,1,0:T(8,128)(2,1)S(1)}, bf16[4,16,512]{2,1,0:T(8,128)(2,1)}, u32[]{:S(2)}) copy-start(bf16[4,16,512]{2,1,0:T(8,128)(2,1)} %reshape.51) | copy-start | bytes 196612
  250.0 48.6 %copy-start.4 = (f32[4,16,512]{2,1,0:T(8,128)S(1)}, f32[4,16,512]{2,1,0:T(8,128)}, u32[]{:S(2)}) copy-start(f32[4,16,512]{2,1,0:T(8,128)} %param.11) | copy-start | bytes 393220
  295.5 6.3 %copy-start.5 = (f32[4,16,512]{2,1,0:T(8,128)S(1)}, f32[4,16,512]{2,1,0:T(8,128)}, u32[]{:S(2)}) copy-start(f32[4,16,512]{2,1,0:T(8,128)} %param.10) | copy-start | bytes 393220
  298.6 3.2 copy-start.1
Sparse Core Ops, SparseCore 0:
  35.1 120.1 reduce-scatter.1
  177.3 70.2 all-gather.2
  298.7 87.8 all-gather.4
where the time goes:
time: 399 us; the launch traced here: 397 us
  waiting for transfers between devices  273 us (68%)
  blocking collectives  63.3 us (16%)
  local copies, waits for them, and re-layouts  27.9 us (7%)
  matrix products  14 us (4%)
  between operations  13.9 us (3%)
  other arithmetic  4.15 us (1%)
    reduce_scatter x1, waiting for transfers between devices, on_device(): lax.psum_scatter(lax.dot_general(columns, my_dout, (((0,), (0,)), ((), ()...  119 us
    all_gather x1, waiting for transfers between devices, on_device(): gathered = lax.all_gather(result, 'owner', axis=0, tiled=True)  83.5 us
    all_gather x1, waiting for transfers between devices, on_device(): shard_rows = lax.all_gather(own_grad, 'dp', axis=1, tiled=True)  70.2 us
    psum x1, blocking collectives, on_device(): pre_sq = lax.psum(jnp.sum(precise * precise, axis=(1, 2)), 'dp')  45.5 us
    all_to_all x1, blocking collectives, on_device(): lax.all_to_all(outgoing.reshape(owner_size, slot_count, tile_size), 'owne...  17.8 us
    unnamed x20, local copies, waits for them, and re-layouts  13.1 us
    transpose x1, local copies, waits for them, and re-layouts, on_device(): columns = columns.reshape(tokens, row_blocks, spread, row_share).transpos...  8.56 us
  transfers between devices with their start and end apart: 3, of which 3 were waited for; matrix products, arithmetic and copies ran while one was open for 1% of the time, Pallas kernels for 0%

commit v1 on v0

v1 whole, which is shorter than its diff:
```python
import functools

import jax
import jax.numpy as jnp
from jax import lax
from jax.experimental import pallas as pl
from jax.experimental.pallas import tpu as pltpu
from jax.sharding import PartitionSpec as P

WARMUP = 25
MESH = pl.DeviceIdType.MESH
LANES = 128
RING_GROUPS = 2
STOP = {1: 0, 2: 1, 3: 0, 4: 3, 5: 3, 6: 0, 7: 6, 8: 6}

decay_rate = 0.95
epsilon = 1e-06


def far_first(k, size):
    odd = lax.rem(k, 2)
    return lax.rem(size // 2 + size + odd * ((k + 1) // 2) - (1 - odd) * (k // 2), size)


def place_tables(owner_row, counter_row, slot_count, col_blocks):
    total = owner_row.shape[1]
    square = (total, total)
    down = lax.broadcasted_iota(jnp.int32, square, 0)
    across = lax.broadcasted_iota(jnp.int32, square, 1)

    def upright(row):
        return jnp.sum(jnp.where(down == across, row, 0), axis=1, keepdims=True)

    owner_col, counter_col = upright(owner_row), upright(counter_row)
    same = owner_col == owner_row
    slot_col = jnp.sum(jnp.where(same & (across < down), 1, 0), axis=1, keepdims=True)
    slot_row = jnp.sum(jnp.where(same & (down < across), 1, 0), axis=0, keepdims=True)
    block_col, block_row = down[:, :1], across[:1, :]
    last = col_blocks - 1
    taken = (block_col & ~last) + ((slot_col - block_col) & last)
    given = owner_row * col_blocks + ((block_row - slot_row) & last)
    places = lax.broadcasted_iota(jnp.int32, (total, LANES), 1)
    hit = owner_col * slot_count + slot_col == places
    source = total + jnp.sum(jnp.where(hit, taken - total, 0), axis=0, keepdims=True)
    begun = jnp.sum(jnp.where(hit & (counter_col >= WARMUP), 1, 0), axis=0, keepdims=True)
    return source, given, begun


def step_kernel(
    owner_hbm,
    counter_hbm,
    dout_hbm,
    acts_hbm,
    left_root_hbm,
    right_root_hbm,
    left_prod,
    right_prod,
    update,
    owner_v,
    counter_v,
    table_v,
    table,
    acts_v,
    dout_v,
    left_root,
    roots,
    right_root,
    terms,
    sibling_terms,
    sum_out,
    sum_in,
    turned,
    tile_out,
    tile_in,
    own_grad,
    grads,
    flipped,
    pre_out,
    precond,
    prod_out,
    prod_in,
    norm_out,
    norm_in,
    pre_tiles,
    grad_tiles,
    result_out,
    result_in,
    returned,
    acts_sem,
    load_sem,
    pair_send,
    pair_recv,
    ring_send,
    ring_recv,
    tile_send,
    tile_recv,
    gather_send,
    gather_recv,
    swap_send,
    swap_recv,
    norm_send,
    norm_recv,
    result_send,
    result_recv,
):
    replica = lax.axis_index("dp")
    owner = lax.axis_index("owner")
    replicas = grads.shape[0]
    owners = tile_in.shape[0]
    chips = replicas // 2
    half = chips // 2
    chip = replica // 2
    core = lax.rem(replica, 2)
    row_blocks, tokens, order = acts_v.shape
    slots, rows, _ = own_grad.shape
    col_blocks = turned.shape[0] // row_blocks
    share = LANES // col_blocks
    group_rows = row_blocks // RING_GROUPS
    kept = slots // 2
    mine = pl.ds(core * kept, kept)
    theirs = pl.ds((1 - core) * kept, kept)
    f32, bf16 = jnp.float32, jnp.bfloat16

    def acts_copy(i):
        return pltpu.make_async_copy(
            acts_hbm.at[:, pl.ds(pl.multiple_of(i * order, order), order)],
            acts_v.at[i],
            acts_sem.at[i],
        )

    dout_copy = pltpu.make_async_copy(dout_hbm, dout_v, load_sem.at[0])
    left_copy = pltpu.make_async_copy(left_root_hbm, left_root, load_sem.at[1])
    right_copy = pltpu.make_async_copy(right_root_hbm.at[mine], right_root, load_sem.at[2])
    owner_copy = pltpu.make_async_copy(owner_hbm, owner_v, load_sem.at[3])
    counter_copy = pltpu.make_async_copy(counter_hbm, counter_v, load_sem.at[4])
    table_copy = pltpu.make_async_copy(table_v, table, load_sem.at[5])
    owner_copy.start()
    counter_copy.start()
    dout_copy.start()
    for i in range(row_blocks):
        acts_copy(i).start()
    left_copy.start()
    right_copy.start()

    across = min(4, owners)

    def owner_peer(k):
        along = far_first(k // across, owners // across)
        aside = far_first(lax.rem(k, across), across)
        y = lax.rem(owner // across + along, owners // across)
        return y * across + lax.rem(lax.rem(owner, across) + aside, across)

    def replica_peer(k):
        there = lax.rem(chip + far_first(k // 2, chips), chips)
        return there * 2 + lax.rem(core + 1 - lax.rem(k, 2), 2)

    barrier = pltpu.get_barrier_semaphore()

    def greet_owner(k, carry):
        peer = owner_peer(k)
        pl.semaphore_signal(barrier, inc=1, device_id=(replica, peer), device_id_type=MESH)
        return carry

    def greet_replica(k, carry):
        peer = replica_peer(k)
        pl.semaphore_signal(barrier, inc=1, device_id=(peer, owner), device_id_type=MESH)
        return carry

    lax.fori_loop(0, replicas - 1, greet_replica, 0)
    lax.fori_loop(0, owners - 1, greet_owner, 0)
    turned[row_blocks * col_blocks] = jnp.zeros((rows, LANES), f32)
    owner_copy.wait()
    counter_copy.wait()
    source, given, begun = place_tables(owner_v[...], counter_v[...], slots, col_blocks)
    table_v[0:1, :] = source
    table_v[1:2, 0 : row_blocks * col_blocks] = given
    table_v[2:3, :] = begun
    table_copy.start()
    dout_copy.wait()

    sibling = (chip * 2 + 1 - core, owner)
    up = (lax.rem(chip + 1, chips) * 2 + core, owner)
    down = (lax.rem(chip + chips - 1, chips) * 2 + core, owner)

    def pair_copy(i):
        return pltpu.make_async_remote_copy(
            src_ref=terms.at[i, :, 1 - core],
            dst_ref=sibling_terms.at[i],
            send_sem=pair_send.at[i],
            recv_sem=pair_recv.at[i],
            device_id=sibling,
            device_id_type=MESH,
        )

    def term_step(i, carry):
        acts_copy(i).wait()
        part = jnp.dot(dout_v[...], acts_v[i], preferred_element_type=f32)
        terms[i] = part.T.astype(bf16).reshape(chips, 2, rows, LANES)
        return carry

    lax.fori_loop(0, row_blocks, term_step, 0)
    pl.semaphore_wait(barrier, owners + replicas - 2)
    for i in range(row_blocks):
        pair_copy(i).start()

    def swap_copy(which, source, target):
        return pltpu.make_async_remote_copy(
            src_ref=source,
            dst_ref=target,
            send_sem=swap_send.at[which],
            recv_sem=swap_recv.at[which],
            device_id=sibling,
            device_id_type=MESH,
        )

    root_swap = swap_copy(0, left_root.at[theirs], roots.at[core])
    grad_swap = swap_copy(1, own_grad.at[theirs], grads.at[replica])
    pre_swap = swap_copy(2, pre_out.at[1 - core], precond.at[mine])
    prod_swap = swap_copy(3, prod_out.at[1 - core], prod_in)
    left_copy.wait()
    root_swap.start()
    roots[core] = left_root[mine]

    def sum_copy(way, group, hops):
        step = hops - STOP[hops]
        peer = lax.rem(chip + (chips - step if way else step), chips) * 2 + core
        return pltpu.make_async_remote_copy(
            src_ref=sum_out.at[way, group, hops],
            dst_ref=sum_in.at[way, group, hops],
            send_sem=ring_send.at[way, group, hops],
            recv_sem=ring_recv.at[way, group, hops],
            device_id=(peer, owner),
            device_id_type=MESH,
        )

    def chip_terms(group, piece):
        here = pl.ds(group * group_rows, group_rows)
        return terms[here, piece, core].astype(f32) + sibling_terms[here, piece].astype(f32)

    def arrived(way, group, hops):
        sum_copy(way, group, hops).wait_recv()
        return sum_in[way, group, hops].astype(f32)

    def pass_on(way, group, hops):
        total = chip_terms(group, lax.rem(chip + (chips - hops if way else hops), chips))
        for other in routes[way]:
            if STOP[other] == hops:
                total = total + arrived(way, group, other)
        sum_out[way, group, hops] = total.astype(bf16)
        sum_copy(way, group, hops).start()

    routes = [range(1, half + 1), range(1, half)]
    for group in range(RING_GROUPS):
        for i in range(group * group_rows, (group + 1) * group_rows):
            pair_copy(i).wait_recv()
        for hops in range(half, 0, -1):
            for way in range(2):
                if hops in routes[way] and STOP[hops]:
                    pass_on(way, group, hops)
    for group in range(RING_GROUPS):
        for hops in range(half, 0, -1):
            for way in range(2):
                if hops in routes[way] and not STOP[hops]:
                    pass_on(way, group, hops)

    for group in range(RING_GROUPS):
        total = chip_terms(group, chip)
        for hops in range(1, half + 1):
            for way in range(2):
                if hops in routes[way] and not STOP[hops]:
                    total = total + arrived(way, group, hops)
        total = total.astype(bf16).astype(f32)
        for i in range(group_rows):
            for k in range(col_blocks):
                tile = total[i] if k == 0 else pltpu.roll(total[i], k * share, 1)
                turned[(group * group_rows + i) * col_blocks + k] = tile

    lane_block = lax.broadcasted_iota(jnp.int32, (rows, LANES), 1) // share

    table_copy.wait()

    def tile_copy(peer):
        return pltpu.make_async_remote_copy(
            src_ref=tile_out.at[peer],
            dst_ref=tile_in.at[owner],
            send_sem=tile_send,
            recv_sem=tile_recv,
            device_id=(replica, peer),
            device_id_type=MESH,
        )

    def tiles_for(peer):
        tile = jnp.zeros((rows, LANES), f32)
        for s in range(slots):
            tile = jnp.where(lane_block == s, turned[table[0, peer * slots + s]], tile)
        return tile.astype(bf16)

    def tile_step(k, carry):
        peer = owner_peer(k)
        tile_out[peer] = tiles_for(peer)
        tile_copy(peer).start()
        return carry

    lax.fori_loop(0, owners - 1, tile_step, 0)
    tile_in[owner] = tiles_for(owner)
    others = pl.ds(0, owners - 1)
    pltpu.make_async_copy(tile_in.at[others], tile_in.at[others], tile_recv).wait()

    pieces = [tile_in[o].astype(f32) for o in range(owners)]
    for s in range(slots):
        for q in range(order // LANES):
            tile = jnp.zeros((rows, LANES), f32)
            for k in range(col_blocks):
                shift = (k - s) * share % LANES
                piece = pieces[q * col_blocks + k]
                piece = pltpu.roll(piece, shift, 1) if shift else piece
                tile = jnp.where(lane_block == k, piece, tile)
            own_grad[s, :, q * LANES : (q + 1) * LANES] = tile.astype(bf16)
    grad_swap.start()
    grads[replica] = own_grad[mine]

    def gather_copy(way, step):
        there = lax.rem(chip + step if way else chip + chips - step, chips)
        piece = grads.at[pl.ds(there * 2, 2)]
        return pltpu.make_async_remote_copy(
            src_ref=piece,
            dst_ref=piece,
            send_sem=gather_send.at[way, step],
            recv_sem=gather_recv.at[way, step],
            device_id=down if way else up,
            device_id_type=MESH,
        )

    grad_swap.wait_recv()
    gather_copy(0, 0).start()
    if half > 1:
        gather_copy(1, 0).start()

    def gather_round(step, carry):
        for way in range(2):
            gather_copy(way, step - 1).wait_recv()
            gather_copy(way, step).start()
        return carry

    lax.fori_loop(1, half - 1, gather_round, 0)
    if half > 1:
        gather_copy(0, half - 2).wait_recv()
        gather_copy(0, half - 1).start()
    root_swap.wait_recv()
    right_copy.wait()
    if half > 1:
        gather_copy(1, half - 2).wait_recv()
    gather_copy(0, half - 1).wait_recv()

    lane = lax.broadcasted_iota(jnp.int32, (1, LANES), 1)
    norms = jnp.zeros((1, LANES), f32)
    for t in range(kept):
        whole = grads[:, t].reshape(order, order)
        root = roots[:, t].reshape(2 * rows, order)
        inner = jnp.dot(root, whole, preferred_element_type=f32).astype(bf16)
        pre = jnp.dot(inner, right_root[t], preferred_element_type=f32).astype(bf16)
        pre_out[:, t] = pre.reshape(2, rows, order)
        pre = pre.astype(f32)
        square = jnp.sum(pre * pre, axis=(0, 1), keepdims=True)
        norms = jnp.where(lane == core * kept + t, square, norms)
    for s in range(slots):
        own = own_grad[s].astype(f32)
        square = jnp.sum(own * own, axis=(0, 1), keepdims=True)
        norms = jnp.where(lane == slots + s, square, norms)
    norm_out[...] = norms

    def norm_copy(peer):
        return pltpu.make_async_remote_copy(
            src_ref=norm_out,
            dst_ref=norm_in.at[replica],
            send_sem=norm_send,
            recv_sem=norm_recv,
            device_id=(peer, owner),
            device_id_type=MESH,
        )

    def norm_step(k, carry):
        norm_copy(replica_peer(k)).start()
        return carry

    lax.fori_loop(0, replicas - 1, norm_step, 0)
    pre_swap.start()
    norm_in[replica] = norms
    precond[mine] = pre_out[core]
    pre_swap.wait_recv()

    for q in range(order // LANES):
        here = slice(q * LANES, (q + 1) * LANES)
        pre_parts = [precond[s, :, here].astype(f32) for s in range(slots)]
        own_parts = [own_grad[s, :, here].astype(f32) for s in range(slots)]
        for k in range(col_blocks):
            pre_tile = jnp.zeros((rows, LANES), f32)
            own_tile = jnp.zeros((rows, LANES), f32)
            for s in range(slots):
                shift = (s - k) * share % LANES
                pre_part, own_part = pre_parts[s], own_parts[s]
                if shift:
                    pre_part = pltpu.roll(pre_part, shift, 1)
                    own_part = pltpu.roll(own_part, shift, 1)
                pre_tile = jnp.where(lane_block == s, pre_part, pre_tile)
                own_tile = jnp.where(lane_block == s, own_part, own_tile)
            pre_tiles[q * col_blocks + k] = pre_tile
            grad_tiles[q * col_blocks + k] = own_tile

    other_replicas = pl.ds(0, replicas - 1)
    pltpu.make_async_copy(
        norm_in.at[other_replicas], norm_in.at[other_replicas], norm_recv
    ).wait()
    norms = jnp.sum(norm_in[...], axis=0)
    scale = jnp.zeros((1, LANES), f32)
    started = jnp.zeros((1, LANES), jnp.int32)
    for s in range(slots):
        graft = jnp.sqrt(norms[:, slots + s : slots + s + 1] / (norms[:, s : s + 1] + epsilon))
        scale = jnp.where(lane // share == s, graft, scale)
        started = jnp.where(lane // share == s, table[2, owner * slots + s], started)

    def result_copy(peer):
        return pltpu.make_async_remote_copy(
            src_ref=result_out.at[peer],
            dst_ref=result_in.at[owner],
            send_sem=result_send,
            recv_sem=result_recv,
            device_id=(replica, peer),
            device_id_type=MESH,
        )

    def result_for(peer):
        return jnp.where(started > 0, pre_tiles[peer] * scale, grad_tiles[peer]).astype(bf16)

    def result_step(k, carry):
        peer = owner_peer(k)
        result_out[peer] = result_for(peer)
        result_copy(peer).start()
        return carry

    lax.fori_loop(0, owners - 1, result_step, 0)
    result_in[owner] = result_for(owner)

    span = pl.ds(pl.multiple_of(chip * 2 * rows // LANES * LANES, LANES), LANES)
    for t in range(kept):
        whole = grads[:, t].reshape(order, order)
        both = grads[pl.ds(chip * 2, 2), t].reshape(2 * rows, order)
        left = lax.dot_general(
            both, whole, (((1,), (1,)), ((), ())), preferred_element_type=f32
        )
        columns = grads[:, t, :, span].reshape(order, LANES)
        flipped[t] = columns.T.reshape(LANES // (2 * rows), 2 * rows, order)
        turned_rows = flipped[t, lax.rem(chip, LANES // (2 * rows))]
        right = jnp.dot(turned_rows, whole, preferred_element_type=f32)
        prod_out[:, 0, t] = left.reshape(2, rows, order)
        prod_out[:, 1, t] = right.reshape(2, rows, order)
    prod_swap.start()
    left_prod[mine] = prod_out[core, 0]
    right_prod[mine] = prod_out[core, 1]

    pltpu.make_async_copy(result_in.at[others], result_in.at[others], result_recv).wait()

    def turn_step(o, carry):
        tile = result_in[o].astype(f32)
        for k in range(col_blocks):
            returned[o * col_blocks + k] = pltpu.roll(tile, k * share, 1) if k else tile
        return carry

    lax.fori_loop(0, owners, turn_step, 0)

    def update_step(i, carry):
        tile = jnp.zeros((rows, LANES), f32)
        for j in range(col_blocks):
            tile = jnp.where(lane_block == j, returned[table[1, i * col_blocks + j]], tile)
        update[i] = tile.astype(bf16)
        return carry

    lax.fori_loop(0, row_blocks, update_step, 0)

    prod_swap.wait_recv()
    left_prod[theirs] = prod_in[0]
    right_prod[theirs] = prod_in[1]

    root_swap.wait_send()
    grad_swap.wait_send()
    pre_swap.wait_send()
    prod_swap.wait_send()
    for i in range(row_blocks):
        pair_copy(i).wait_send()

    def sent(step, carry):
        for way in range(2):
            gather_copy(way, step).wait_send()
        return carry

    lax.fori_loop(0, half - 1, sent, 0)
    for way in range(2):
        for group in range(RING_GROUPS):
            for hops in routes[way]:
                sum_copy(way, group, hops).wait_send()
    gather_copy(0, half - 1).wait_send()
    pltpu.make_async_copy(tile_in.at[others], tile_in.at[others], tile_send).wait()
    pltpu.make_async_copy(
        norm_in.at[other_replicas], norm_in.at[other_replicas], norm_send
    ).wait()
    pltpu.make_async_copy(result_in.at[others], result_in.at[others], result_send).wait()


def finish_kernel(
    left_stats,
    right_stats,
    left_prod,
    right_prod,
    tiles,
    left_out,
    right_out,
    update,
    left_v,
    right_v,
    left_prod_v,
    right_prod_v,
    tiles_v,
    load_sem,
):
    col_blocks, share = update.shape[2:]
    sources = (tiles, left_stats, left_prod, right_stats, right_prod)
    targets = (tiles_v, left_v, left_prod_v, right_v, right_prod_v)
    copies = [
        pltpu.make_async_copy(source, target, load_sem.at[i])
        for i, (source, target) in enumerate(zip(sources, targets))
    ]
    for copy in copies:
        copy.start()
    copies[0].wait()
    for j in range(col_blocks):
        update[:, :, j, :] = tiles_v[:, :, j * share : (j + 1) * share]
    copies[1].wait()
    copies[2].wait()
    left_out[...] = decay_rate * left_v[...] + (1.0 - decay_rate) * left_prod_v[...]
    copies[3].wait()
    copies[4].wait()
    right_out[...] = decay_rate * right_v[...] + (1.0 - decay_rate) * right_prod_v[...]


def on_device(acts, dout, left_stats, right_stats, left_root, right_root, owner_of, counters):
    replicas, owners = lax.axis_size("dp"), lax.axis_size("owner")
    tokens, features = acts.shape
    col_blocks, share = dout.shape[1:]
    slots, rows, order = left_stats.shape
    row_blocks = features // order
    chips = replicas // 2
    half = chips // 2
    f32, bf16 = jnp.float32, jnp.bfloat16
    total = counters.shape[0]
    dout_rows = dout.transpose(1, 2, 0).reshape(col_blocks * share, tokens)
    vmem = functools.partial(pl.BlockSpec, memory_space=pltpu.VMEM)
    anywhere = functools.partial(pl.BlockSpec, memory_space=pl.ANY)
    kept = slots // 2
    ring_shape = (2, RING_GROUPS, half + 1, row_blocks // RING_GROUPS, rows, LANES)
    dma = pltpu.SemaphoreType.DMA
    left_prod, right_prod, update = pl.pallas_call(
        step_kernel,
        out_shape=(
            jax.ShapeDtypeStruct((slots, rows, order), f32),
            jax.ShapeDtypeStruct((slots, rows, order), f32),
            jax.ShapeDtypeStruct((row_blocks, rows, LANES), bf16),
        ),
        in_specs=[anywhere()] * 6,
        out_specs=(vmem(), vmem(), vmem()),
        scratch_shapes=[
            pltpu.VMEM((1, total), jnp.int32),
            pltpu.VMEM((1, total), jnp.int32),
            pltpu.VMEM((8, LANES), jnp.int32),
            pltpu.SMEM((8, LANES), jnp.int32),
            pltpu.VMEM((row_blocks, tokens, order), bf16),
            pltpu.VMEM((LANES, tokens), bf16),
            pltpu.VMEM((slots, rows, order), bf16),
            pltpu.VMEM((2, kept, rows, order), bf16),
            pltpu.VMEM((kept, order, order), bf16),
            pltpu.VMEM((row_blocks, chips, 2, rows, LANES), bf16),
            pltpu.VMEM((row_blocks, chips, rows, LANES), bf16),
            pltpu.VMEM(ring_shape, bf16),
            pltpu.VMEM(ring_shape, bf16),
            pltpu.VMEM((row_blocks * col_blocks + 1, rows, LANES), f32),
            pltpu.VMEM((owners, rows, LANES), bf16),
            pltpu.VMEM((owners, rows, LANES), bf16),
            pltpu.VMEM((slots, rows, order), bf16),
            pltpu.VMEM((replicas, kept, rows, order), bf16),
            pltpu.VMEM((kept, LANES // (2 * rows), 2 * rows, order), bf16),
            pltpu.VMEM((2, kept, rows, order), bf16),
            pltpu.VMEM((slots, rows, order), bf16),
            pltpu.VMEM((2, 2, kept, rows, order), f32),
            pltpu.VMEM((2, kept, rows, order), f32),
            pltpu.VMEM((1, LANES), f32),
            pltpu.VMEM((replicas, 1, LANES), f32),
            pltpu.VMEM((owners, rows, LANES), f32),
            pltpu.VMEM((owners, rows, LANES), f32),
            pltpu.VMEM((owners, rows, LANES), bf16),
            pltpu.VMEM((owners, rows, LANES), bf16),
            pltpu.VMEM((owners * col_blocks, rows, LANES), f32),
            dma((row_blocks,)),
            dma((6,)),
            dma((row_blocks,)),
            dma((row_blocks,)),
            dma((2, RING_GROUPS, half + 1)),
            dma((2, RING_GROUPS, half + 1)),
            dma,
            dma,
            dma((2, half)),
            dma((2, half)),
            dma((4,)),
            dma((4,)),
            dma,
            dma,
            dma,
            dma,
        ],
        compiler_params=pltpu.CompilerParams(
            collective_id=0, has_side_effects=True, vmem_limit_bytes=56 * 1024 * 1024
        ),
    )(owner_of.reshape(1, total), counters.reshape(1, total), dout_rows, acts, left_root, right_root)
    return pl.pallas_call(
        finish_kernel,
        out_shape=(
            jax.ShapeDtypeStruct((slots, rows, order), f32),
            jax.ShapeDtypeStruct((slots, rows, order), f32),
            jax.ShapeDtypeStruct((row_blocks, rows, col_blocks, share), bf16),
        ),
        in_specs=[anywhere()] * 5,
        out_specs=(vmem(), vmem(), vmem()),
        scratch_shapes=[pltpu.VMEM((slots, rows, order), f32)] * 4
        + [pltpu.VMEM((row_blocks, rows, LANES), bf16), dma((5,))],
    )(left_stats, right_stats, left_prod, right_prod, update)


def solution(mesh):
    in_specs = (
        P("dp", None),
        P("dp", None, "owner"),
        P("owner", "dp", None),
        P("owner", "dp", None),
        P("owner", "dp", None),
        P("owner", None, None),
        P(),
        P(),
    )
    out_specs = (P("owner", "dp", None), P("owner", "dp", None), P(None, "dp", None, "owner"))
    return jax.shard_map(
        on_device, mesh=mesh, in_specs=in_specs, out_specs=out_specs, check_vma=False
    )
```

time: 399 us -> 99.5 us (0.25)
  waiting for transfers between devices: 273 us -> 0 us
  Pallas kernels: 0 us -> 98.7 us
  blocking collectives: 63.3 us -> 0 us
  local copies, waits for them, and re-layouts: 27.9 us -> 0 us
  matrix products: 14 us -> 0 us
  between operations: 13.9 us -> 0.64 us
  other arithmetic: 4.15 us -> 0 us
    all_gather x2 -> x0, waiting for transfers between devices: 154 us -> none  [the longest x1 83.5 us: on_device(): gathered = lax.all_gather(result, 'owner', axis=0, tiled=True)]
    reduce_scatter x1 -> x0, waiting for transfers between devices: 119 us -> none  [on_device(): lax.psum_scatter(lax.dot_general(columns, my_dout, (((0,), (0,)), ((), ()...]
    pallas_call x0 -> x2, Pallas kernels: none -> 98.7 us  [the longest x1 96.1 us: on_device(): pl.pallas_call(step_kernel, out_shape=(jax.ShapeDtypeStruct((slots, rows,...]
    psum x1 -> x0, blocking collectives: 45.5 us -> none  [on_device(): pre_sq = lax.psum(jnp.sum(precise * precise, axis=(1, 2)), 'dp')]
    all_to_all x1 -> x0, blocking collectives: 17.8 us -> none  [on_device(): lax.all_to_all(outgoing.reshape(owner_size, slot_count, tile_size), 'owne...]
    dot_general x4 -> x0, matrix products: 14 us -> none  [the longest x1 7.12 us: on_device(): lax.dot_general(columns, my_dout, (((0,), (0,)), ((), ())), preferred_ele...]
    unnamed x20 -> x0, local copies, waits for them, and re-layouts: 13.1 us -> none
    transpose x2 -> x0, local copies, waits for them, and re-layouts: 8.85 us -> none  [the longest x1 8.56 us: on_device(): columns = columns.reshape(tokens, row_blocks, spread, row_share).transpos...]
  transfers between devices with their start and end apart: 3 -> 0, of which waited for: 3 -> 0; matrix products, arithmetic and copies ran while one was open for 1% -> 0% of each run, Pallas kernels for 0% -> 0%
where the time goes in v1:
time: 99.5 us; the launch traced here: 99.4 us
  Pallas kernels  98.7 us (99%)
    pallas_call x1, Pallas kernels, on_device(): pl.pallas_call(step_kernel, out_shape=(jax.ShapeDtypeStruct((slots, rows,...  96.1 us
    pallas_call x1, Pallas kernels, on_device(): pl.pallas_call(finish_kernel, out_shape=(jax.ShapeDtypeStruct((slots, row...  2.64 us

profile of v1, /device:TPU:1, one launch (start us, length us, event | category | flops | bytes accessed | tf_op | source)
XLA Modules:
  0.0 99.4 jit_solution(7444991933584417946)
XLA Ops:
  0.6 96.1 %shard_map.103 = (f32[4,16,512]{2,1,0:T(8,128)}, f32[4,16,512]{2,1,0:T(8,128)}, bf16[8,16,128]{2,1,0:T(8,128)(2,1)}) custom-call(s32[1,64]{1,0:T(1,128)} %bitcast.6, s32[1,64]{1,0:T(1,128)} %bitcast.7, bf16[128,1024]{1,0:T(8,128)(2,1)} %bitcast.5, bf16[1024,4096]{1,0:T(8,128)(2,1)} %acts_hbm.1, bf16[4,16,512]{2,1,0:T(8,128)(2,1)} %left_root_hbm.1, ...), custom_call_target="tpu_custom_call" | custom-call | tf_op jit(solution)/shard_map/pallas_call | solution.py:561
  96.7 2.6 %shard_map.104 = (f32[4,16,512]{2,1,0:T(8,128)}, f32[4,16,512]{2,1,0:T(8,128)}, bf16[8,16,8,16]{3,2,1,0:T(8,128)(2,1)}) custom-call(f32[4,16,512]{2,1,0:T(8,128)} %left_stats.1, f32[4,16,512]{2,1,0:T(8,128)} %right_stats.1, f32[4,16,512]{2,1,0:T(8,128)} %get-tuple-element.6.left_prod, f32[4,16,512]{2,1,0:T(8,128)} %get-tuple-element.7.right_prod, ...), custom_call_target="tpu_custom_call" | custom-call | tf_op jit(solution)/shard_map/pallas_call | solution.py:622

commit v2 on v1

--- a/solution.py
+++ b/solution.py
@@ -17,9 +17,22 @@
 epsilon = 1e-06
 
 
-def far_first(k, size):
-    odd = lax.rem(k, 2)
-    return lax.rem(size // 2 + size + odd * ((k + 1) // 2) - (1 - odd) * (k // 2), size)
+def around(place, size):
+    place = jnp.where(place >= size, place - size, place)
+    return jnp.where(place < 0, place + size, place)
+
+
+def far_first(size):
+    return [(size // 2 + ((k + 1) // 2 if k % 2 else -(k // 2))) % size for k in range(size)]
+
+
+def swing(size, visit):
+    def step(k, carry):
+        distance, stride, side = carry
+        visit(distance)
+        return distance + side * stride, stride + 1, -side
+
+    lax.fori_loop(0, size - 1, step, (jnp.int32(size // 2), jnp.int32(1), jnp.int32(1)))
 
 
 def place_tables(owner_row, counter_row, slot_count, col_blocks):
@@ -144,30 +157,38 @@
 
     across = min(4, owners)
 
-    def owner_peer(k):
-        along = far_first(k // across, owners // across)
-        aside = far_first(lax.rem(k, across), across)
-        y = lax.rem(owner // across + along, owners // across)
-        return y * across + lax.rem(lax.rem(owner, across) + aside, across)
-
-    def replica_peer(k):
-        there = lax.rem(chip + far_first(k // 2, chips), chips)
-        return there * 2 + lax.rem(core + 1 - lax.rem(k, 2), 2)
+    high, wide = owner // across, lax.rem(owner, across)
+    beside = [around(wide + d, across) for d in far_first(across)]
+
+    def each_owner(visit):
+        def row(distance):
+            y = around(high + distance, owners // across) * across
+            for x in beside:
+                visit(y + x)
+
+        swing(owners // across, row)
+        for x in beside[:-1]:
+            visit(high * across + x)
+
+    def each_replica(visit):
+        def both(distance):
+            there = around(chip + distance, chips) * 2
+            visit(there)
+            visit(there + 1)
+
+        swing(chips, both)
+        visit(chip * 2 + 1 - core)
 
     barrier = pltpu.get_barrier_semaphore()
 
-    def greet_owner(k, carry):
-        peer = owner_peer(k)
+    def greet_owner(peer):
         pl.semaphore_signal(barrier, inc=1, device_id=(replica, peer), device_id_type=MESH)
-        return carry
-
-    def greet_replica(k, carry):
-        peer = replica_peer(k)
+
+    def greet_replica(peer):
         pl.semaphore_signal(barrier, inc=1, device_id=(peer, owner), device_id_type=MESH)
-        return carry
-
-    lax.fori_loop(0, replicas - 1, greet_replica, 0)
-    lax.fori_loop(0, owners - 1, greet_owner, 0)
+
+    each_replica(greet_replica)
+    each_owner(greet_owner)
     turned[row_blocks * col_blocks] = jnp.zeros((rows, LANES), f32)
     owner_copy.wait()
     counter_copy.wait()
@@ -179,8 +200,8 @@
     dout_copy.wait()
 
     sibling = (chip * 2 + 1 - core, owner)
-    up = (lax.rem(chip + 1, chips) * 2 + core, owner)
-    down = (lax.rem(chip + chips - 1, chips) * 2 + core, owner)
+    up = (around(chip + 1, chips) * 2 + core, owner)
+    down = (around(chip - 1, chips) * 2 + core, owner)
 
     def pair_copy(i):
         return pltpu.make_async_remote_copy(
@@ -223,7 +244,7 @@
 
     def sum_copy(way, group, hops):
         step = hops - STOP[hops]
-        peer = lax.rem(chip + (chips - step if way else step), chips) * 2 + core
+        peer = around(chip + (-step if way else step), chips) * 2 + core
         return pltpu.make_async_remote_copy(
             src_ref=sum_out.at[way, group, hops],
             dst_ref=sum_in.at[way, group, hops],
@@ -242,7 +263,7 @@
         return sum_in[way, group, hops].astype(f32)
 
     def pass_on(way, group, hops):
-        total = chip_terms(group, lax.rem(chip + (chips - hops if way else hops), chips))
+        total = chip_terms(group, around(chip + (-hops if way else hops), chips))
         for other in routes[way]:
             if STOP[other] == hops:
                 total = total + arrived(way, group, other)
@@ -295,13 +316,11 @@
             tile = jnp.where(lane_block == s, turned[table[0, peer * slots + s]], tile)
         return tile.astype(bf16)
 
-    def tile_step(k, carry):
-        peer = owner_peer(k)
+    def tile_step(peer):
         tile_out[peer] = tiles_for(peer)
         tile_copy(peer).start()
-        return carry
-
-    lax.fori_loop(0, owners - 1, tile_step, 0)
+
+    each_owner(tile_step)
     tile_in[owner] = tiles_for(owner)
     others = pl.ds(0, owners - 1)
     pltpu.make_async_copy(tile_in.at[others], tile_in.at[others], tile_recv).wait()
@@ -320,7 +339,7 @@
     grads[replica] = own_grad[mine]
 
     def gather_copy(way, step):
-        there = lax.rem(chip + step if way else chip + chips - step, chips)
+        there = around(chip + (step if way else -step), chips)
         piece = grads.at[pl.ds(there * 2, 2)]
         return pltpu.make_async_remote_copy(
             src_ref=piece,
@@ -379,11 +398,10 @@
             device_id_type=MESH,
         )
 
-    def norm_step(k, carry):
-        norm_copy(replica_peer(k)).start()
-        return carry
-
-    lax.fori_loop(0, replicas - 1, norm_step, 0)
+    def norm_step(peer):
+        norm_copy(peer).start()
+
+    each_replica(norm_step)
     pre_swap.start()
     norm_in[replica] = norms
     precond[mine] = pre_out[core]
@@ -432,13 +450,11 @@
     def result_for(peer):
         return jnp.where(started > 0, pre_tiles[peer] * scale, grad_tiles[peer]).astype(bf16)
 
-    def result_step(k, carry):
-        peer = owner_peer(k)
+    def result_step(peer):
         result_out[peer] = result_for(peer)
         result_copy(peer).start()
-        return carry
-
-    lax.fori_loop(0, owners - 1, result_step, 0)
+
+    each_owner(result_step)
     result_in[owner] = result_for(owner)
 
     span = pl.ds(pl.multiple_of(chip * 2 * rows // LANES * LANES, LANES), LANES)

time: 99.5 us -> 98.4 us (0.989)
  Pallas kernels: 98.7 us -> 97.6 us
    pallas_call x1, Pallas kernels: 96.1 us -> 94.9 us  [on_device(): pl.pallas_call(step_kernel, out_shape=(jax.ShapeDtypeStruct((slots, rows,...]
where the time goes in v2:
time: 98.4 us; the launch traced here: 98.2 us
  Pallas kernels  97.6 us (99%)
    pallas_call x1, Pallas kernels, on_device(): pl.pallas_call(step_kernel, out_shape=(jax.ShapeDtypeStruct((slots, rows,...  94.9 us
    pallas_call x1, Pallas kernels, on_device(): pl.pallas_call(finish_kernel, out_shape=(jax.ShapeDtypeStruct((slots, row...  2.64 us

profile of v2, /device:TPU:1, one launch (start us, length us, event | category | flops | bytes accessed | tf_op | source)
XLA Modules:
  0.0 98.2 jit_solution(11939715745580380068)
XLA Ops:
  0.6 94.9 %shard_map.103 = (f32[4,16,512]{2,1,0:T(8,128)}, f32[4,16,512]{2,1,0:T(8,128)}, bf16[8,16,128]{2,1,0:T(8,128)(2,1)}) custom-call(s32[1,64]{1,0:T(1,128)} %bitcast.6, s32[1,64]{1,0:T(1,128)} %bitcast.7, bf16[128,1024]{1,0:T(8,128)(2,1)} %bitcast.5, bf16[1024,4096]{1,0:T(8,128)(2,1)} %acts_hbm.1, bf16[4,16,512]{2,1,0:T(8,128)(2,1)} %left_root_hbm.1, ...), custom_call_target="tpu_custom_call" | custom-call | tf_op jit(solution)/shard_map/pallas_call | solution.py:577
  95.6 2.6 %shard_map.104 = (f32[4,16,512]{2,1,0:T(8,128)}, f32[4,16,512]{2,1,0:T(8,128)}, bf16[8,16,8,16]{3,2,1,0:T(8,128)(2,1)}) custom-call(f32[4,16,512]{2,1,0:T(8,128)} %left_stats.1, f32[4,16,512]{2,1,0:T(8,128)} %right_stats.1, f32[4,16,512]{2,1,0:T(8,128)} %get-tuple-element.6.left_prod, f32[4,16,512]{2,1,0:T(8,128)} %get-tuple-element.7.right_prod, ...), custom_call_target="tpu_custom_call" | custom-call | tf_op jit(solution)/shard_map/pallas_call | solution.py:638

commit v3 on v2

--- a/solution.py
+++ b/solution.py
@@ -219,10 +219,17 @@
         terms[i] = part.T.astype(bf16).reshape(chips, 2, rows, LANES)
         return carry
 
-    lax.fori_loop(0, row_blocks, term_step, 0)
+    def term_and_pair(i, carry):
+        term_step(i, carry)
+        pair_copy(i).start()
+        return carry
+
+    early = row_blocks * 3 // 4
+    lax.fori_loop(0, early, term_step, 0)
     pl.semaphore_wait(barrier, owners + replicas - 2)
-    for i in range(row_blocks):
+    for i in range(early):
         pair_copy(i).start()
+    lax.fori_loop(early, row_blocks, term_and_pair, 0)
 
     def swap_copy(which, source, target):
         return pltpu.make_async_remote_copy(
@@ -355,6 +362,13 @@
     if half > 1:
         gather_copy(1, 0).start()
 
+    lane = lax.broadcasted_iota(jnp.int32, (1, LANES), 1)
+    norms = jnp.zeros((1, LANES), f32)
+    for s in range(slots):
+        own = own_grad[s].astype(f32)
+        square = jnp.sum(own * own, axis=(0, 1), keepdims=True)
+        norms = jnp.where(lane == slots + s, square, norms)
+
     def gather_round(step, carry):
         for way in range(2):
             gather_copy(way, step - 1).wait_recv()
@@ -371,8 +385,6 @@
         gather_copy(1, half - 2).wait_recv()
     gather_copy(0, half - 1).wait_recv()
 
-    lane = lax.broadcasted_iota(jnp.int32, (1, LANES), 1)
-    norms = jnp.zeros((1, LANES), f32)
     for t in range(kept):
         whole = grads[:, t].reshape(order, order)
         root = roots[:, t].reshape(2 * rows, order)
@@ -382,10 +394,6 @@
         pre = pre.astype(f32)
         square = jnp.sum(pre * pre, axis=(0, 1), keepdims=True)
         norms = jnp.where(lane == core * kept + t, square, norms)
-    for s in range(slots):
-        own = own_grad[s].astype(f32)
-        square = jnp.sum(own * own, axis=(0, 1), keepdims=True)
-        norms = jnp.where(lane == slots + s, square, norms)
     norm_out[...] = norms
 
     def norm_copy(peer):
@@ -405,6 +413,24 @@
     pre_swap.start()
     norm_in[replica] = norms
     precond[mine] = pre_out[core]
+
+    span = pl.ds(pl.multiple_of(chip * 2 * rows // LANES * LANES, LANES), LANES)
+    for t in range(kept):
+        whole = grads[:, t].reshape(order, order)
+        both = grads[pl.ds(chip * 2, 2), t].reshape(2 * rows, order)
+        left = lax.dot_general(
+            both, whole, (((1,), (1,)), ((), ())), preferred_element_type=f32
+        )
+        columns = grads[:, t, :, span].reshape(order, LANES)
+        flipped[t] = columns.T.reshape(LANES // (2 * rows), 2 * rows, order)
+        turned_rows = flipped[t, lax.rem(chip, LANES // (2 * rows))]
+        right = jnp.dot(turned_rows, whole, preferred_element_type=f32)
+        prod_out[:, 0, t] = left.reshape(2, rows, order)
+        prod_out[:, 1, t] = right.reshape(2, rows, order)
+    prod_swap.start()
+    left_prod[mine] = prod_out[core, 0]
+    right_prod[mine] = prod_out[core, 1]
+
     pre_swap.wait_recv()
 
     for q in range(order // LANES):
@@ -456,23 +482,6 @@
 
     each_owner(result_step)
     result_in[owner] = result_for(owner)
-
-    span = pl.ds(pl.multiple_of(chip * 2 * rows // LANES * LANES, LANES), LANES)
-    for t in range(kept):
-        whole = grads[:, t].reshape(order, order)
-        both = grads[pl.ds(chip * 2, 2), t].reshape(2 * rows, order)
-        left = lax.dot_general(
-            both, whole, (((1,), (1,)), ((), ())), preferred_element_type=f32
-        )
-        columns = grads[:, t, :, span].reshape(order, LANES)
-        flipped[t] = columns.T.reshape(LANES // (2 * rows), 2 * rows, order)
-        turned_rows = flipped[t, lax.rem(chip, LANES // (2 * rows))]
-        right = jnp.dot(turned_rows, whole, preferred_element_type=f32)
-        prod_out[:, 0, t] = left.reshape(2, rows, order)
-        prod_out[:, 1, t] = right.reshape(2, rows, order)
-    prod_swap.start()
-    left_prod[mine] = prod_out[core, 0]
-    right_prod[mine] = prod_out[core, 1]
 
     pltpu.make_async_copy(result_in.at[others], result_in.at[others], result_recv).wait()
 

time: 98.4 us -> 98.6 us (level)
  no operation moved by 1% of the time
where the time goes in v3:
time: 98.6 us; the launch traced here: 98.4 us
  Pallas kernels  97.8 us (99%)
    pallas_call x1, Pallas kernels, on_device(): pl.pallas_call(step_kernel, out_shape=(jax.ShapeDtypeStruct((slots, rows,...  95.1 us
    pallas_call x1, Pallas kernels, on_device(): pl.pallas_call(finish_kernel, out_shape=(jax.ShapeDtypeStruct((slots, row...  2.64 us

profile of v3, /device:TPU:1, one launch (start us, length us, event | category | flops | bytes accessed | tf_op | source)
XLA Modules:
  0.0 98.4 jit_solution(2270824954782225886)
XLA Ops:
  0.6 95.1 %shard_map.103 = (f32[4,16,512]{2,1,0:T(8,128)}, f32[4,16,512]{2,1,0:T(8,128)}, bf16[8,16,128]{2,1,0:T(8,128)(2,1)}) custom-call(s32[1,64]{1,0:T(1,128)} %bitcast.6, s32[1,64]{1,0:T(1,128)} %bitcast.7, bf16[128,1024]{1,0:T(8,128)(2,1)} %bitcast.5, bf16[1024,4096]{1,0:T(8,128)(2,1)} %acts_hbm.1, bf16[4,16,512]{2,1,0:T(8,128)(2,1)} %left_root_hbm.1, ...), custom_call_target="tpu_custom_call" | custom-call | tf_op jit(solution)/shard_map/pallas_call | solution.py:586
  95.8 2.6 %shard_map.104 = (f32[4,16,512]{2,1,0:T(8,128)}, f32[4,16,512]{2,1,0:T(8,128)}, bf16[8,16,8,16]{3,2,1,0:T(8,128)(2,1)}) custom-call(f32[4,16,512]{2,1,0:T(8,128)} %left_stats.1, f32[4,16,512]{2,1,0:T(8,128)} %right_stats.1, f32[4,16,512]{2,1,0:T(8,128)} %get-tuple-element.6.left_prod, f32[4,16,512]{2,1,0:T(8,128)} %get-tuple-element.7.right_prod, ...), custom_call_target="tpu_custom_call" | custom-call | tf_op jit(solution)/shard_map/pallas_call | solution.py:647

commit v4 on v3

--- a/solution.py
+++ b/solution.py
@@ -11,7 +11,7 @@
 MESH = pl.DeviceIdType.MESH
 LANES = 128
 RING_GROUPS = 2
-STOP = {1: 0, 2: 1, 3: 0, 4: 3, 5: 3, 6: 0, 7: 6, 8: 6}
+STOP = {1: 0, 2: 0, 3: 2, 4: 2, 5: 0, 6: 5, 7: 5, 8: 5}
 
 decay_rate = 0.95
 epsilon = 1e-06
@@ -485,13 +485,17 @@
 
     pltpu.make_async_copy(result_in.at[others], result_in.at[others], result_recv).wait()
 
-    def turn_step(o, carry):
-        tile = result_in[o].astype(f32)
-        for k in range(col_blocks):
-            returned[o * col_blocks + k] = pltpu.roll(tile, k * share, 1) if k else tile
+    batch = min(8, owners)
+
+    def turn_step(n, carry):
+        for o in range(batch):
+            tile = result_in[n * batch + o].astype(f32)
+            for k in range(col_blocks):
+                place = (n * batch + o) * col_blocks + k
+                returned[place] = pltpu.roll(tile, k * share, 1) if k else tile
         return carry
 
-    lax.fori_loop(0, owners, turn_step, 0)
+    lax.fori_loop(0, owners // batch, turn_step, 0)
 
     def update_step(i, carry):
         tile = jnp.zeros((rows, LANES), f32)

time: 98.6 us -> 96.6 us (0.980)
  Pallas kernels: 97.8 us -> 95.8 us
    pallas_call x1, Pallas kernels: 95.1 us -> 93.2 us  [on_device(): pl.pallas_call(step_kernel, out_shape=(jax.ShapeDtypeStruct((slots, rows,...]
where the time goes in v4:
time: 96.6 us; the launch traced here: 96.5 us
  Pallas kernels  95.8 us (99%)
    pallas_call x1, Pallas kernels, on_device(): pl.pallas_call(step_kernel, out_shape=(jax.ShapeDtypeStruct((slots, rows,...  93.2 us
    pallas_call x1, Pallas kernels, on_device(): pl.pallas_call(finish_kernel, out_shape=(jax.ShapeDtypeStruct((slots, row...  2.64 us

profile of v4, /device:TPU:1, one launch (start us, length us, event | category | flops | bytes accessed | tf_op | source)
XLA Modules:
  0.0 96.5 jit_solution(6689639789380727647)
XLA Ops:
  0.6 93.2 %shard_map.103 = (f32[4,16,512]{2,1,0:T(8,128)}, f32[4,16,512]{2,1,0:T(8,128)}, bf16[8,16,128]{2,1,0:T(8,128)(2,1)}) custom-call(s32[1,64]{1,0:T(1,128)} %bitcast.6, s32[1,64]{1,0:T(1,128)} %bitcast.7, bf16[128,1024]{1,0:T(8,128)(2,1)} %bitcast.5, bf16[1024,4096]{1,0:T(8,128)(2,1)} %acts_hbm.1, bf16[4,16,512]{2,1,0:T(8,128)(2,1)} %left_root_hbm.1, ...), custom_call_target="tpu_custom_call" | custom-call | tf_op jit(solution)/shard_map/pallas_call | solution.py:590
  93.8 2.6 %shard_map.104 = (f32[4,16,512]{2,1,0:T(8,128)}, f32[4,16,512]{2,1,0:T(8,128)}, bf16[8,16,8,16]{3,2,1,0:T(8,128)(2,1)}) custom-call(f32[4,16,512]{2,1,0:T(8,128)} %left_stats.1, f32[4,16,512]{2,1,0:T(8,128)} %right_stats.1, f32[4,16,512]{2,1,0:T(8,128)} %get-tuple-element.6.left_prod, f32[4,16,512]{2,1,0:T(8,128)} %get-tuple-element.7.right_prod, ...), custom_call_target="tpu_custom_call" | custom-call | tf_op jit(solution)/shard_map/pallas_call | solution.py:651

commit v5 on v4

--- a/solution.py
+++ b/solution.py
@@ -163,12 +163,10 @@
     def each_owner(visit):
         def row(distance):
             y = around(high + distance, owners // across) * across
-            for x in beside:
-                visit(y + x)
+            visit([y + x for x in beside])
 
         swing(owners // across, row)
-        for x in beside[:-1]:
-            visit(high * across + x)
+        visit([high * across + x for x in beside[:-1]])
 
     def each_replica(visit):
         def both(distance):
@@ -181,8 +179,9 @@
 
     barrier = pltpu.get_barrier_semaphore()
 
-    def greet_owner(peer):
-        pl.semaphore_signal(barrier, inc=1, device_id=(replica, peer), device_id_type=MESH)
+    def greet_owner(peers):
+        for peer in peers:
+            pl.semaphore_signal(barrier, inc=1, device_id=(replica, peer), device_id_type=MESH)
 
     def greet_replica(peer):
         pl.semaphore_signal(barrier, inc=1, device_id=(peer, owner), device_id_type=MESH)
@@ -323,9 +322,12 @@
             tile = jnp.where(lane_block == s, turned[table[0, peer * slots + s]], tile)
         return tile.astype(bf16)
 
-    def tile_step(peer):
-        tile_out[peer] = tiles_for(peer)
-        tile_copy(peer).start()
+    def tile_step(peers):
+        tiles = [tiles_for(peer) for peer in peers]
+        for peer, tile in zip(peers, tiles):
+            tile_out[peer] = tile
+        for peer in peers:
+            tile_copy(peer).start()
 
     each_owner(tile_step)
     tile_in[owner] = tiles_for(owner)
@@ -476,9 +478,12 @@
     def result_for(peer):
         return jnp.where(started > 0, pre_tiles[peer] * scale, grad_tiles[peer]).astype(bf16)
 
-    def result_step(peer):
-        result_out[peer] = result_for(peer)
-        result_copy(peer).start()
+    def result_step(peers):
+        results = [result_for(peer) for peer in peers]
+        for peer, result in zip(peers, results):
+            result_out[peer] = result
+        for peer in peers:
+            result_copy(peer).start()
 
     each_owner(result_step)
     result_in[owner] = result_for(owner)
@@ -497,14 +502,11 @@
 
     lax.fori_loop(0, owners // batch, turn_step, 0)
 
-    def update_step(i, carry):
+    for i in range(row_blocks):
         tile = jnp.zeros((rows, LANES), f32)
         for j in range(col_blocks):
             tile = jnp.where(lane_block == j, returned[table[1, i * col_blocks + j]], tile)
         update[i] = tile.astype(bf16)
-        return carry
-
-    lax.fori_loop(0, row_blocks, update_step, 0)
 
     prod_swap.wait_recv()
     left_prod[theirs] = prod_in[0]

time: 96.6 us -> 96.4 us (level)
  no operation moved by 1% of the time
where the time goes in v5:
time: 96.4 us; the launch traced here: 96.2 us
  Pallas kernels  95.6 us (99%)
    pallas_call x1, Pallas kernels, on_device(): pl.pallas_call(step_kernel, out_shape=(jax.ShapeDtypeStruct((slots, rows,...  92.9 us
    pallas_call x1, Pallas kernels, on_device(): pl.pallas_call(finish_kernel, out_shape=(jax.ShapeDtypeStruct((slots, row...  2.64 us

profile of v5, /device:TPU:1, one launch (start us, length us, event | category | flops | bytes accessed | tf_op | source)
XLA Modules:
  0.0 96.2 jit_solution(17630612228480890537)
XLA Ops:
  0.6 92.9 %shard_map.103 = (f32[4,16,512]{2,1,0:T(8,128)}, f32[4,16,512]{2,1,0:T(8,128)}, bf16[8,16,128]{2,1,0:T(8,128)(2,1)}) custom-call(s32[1,64]{1,0:T(1,128)} %bitcast.6, s32[1,64]{1,0:T(1,128)} %bitcast.7, bf16[128,1024]{1,0:T(8,128)(2,1)} %bitcast.5, bf16[1024,4096]{1,0:T(8,128)(2,1)} %acts_hbm.1, bf16[4,16,512]{2,1,0:T(8,128)(2,1)} %left_root_hbm.1, ...), custom_call_target="tpu_custom_call" | custom-call | tf_op jit(solution)/shard_map/pallas_call | solution.py:592
  93.5 2.6 %shard_map.104 = (f32[4,16,512]{2,1,0:T(8,128)}, f32[4,16,512]{2,1,0:T(8,128)}, bf16[8,16,8,16]{3,2,1,0:T(8,128)(2,1)}) custom-call(f32[4,16,512]{2,1,0:T(8,128)} %left_stats.1, f32[4,16,512]{2,1,0:T(8,128)} %right_stats.1, f32[4,16,512]{2,1,0:T(8,128)} %get-tuple-element.6.left_prod, f32[4,16,512]{2,1,0:T(8,128)} %get-tuple-element.7.right_prod, ...), custom_call_target="tpu_custom_call" | custom-call | tf_op jit(solution)/shard_map/pallas_call | solution.py:653
